TPU v7x, 32 devices: a whole 2x2x4 slice. The times are simulated.
32 devices in a mesh: axial: 8 (over z, y), azim: 4 (over x, core).
Axes of the slice: x: 2, y: 2, z: 4, core: 2. Of those that a mesh axis runs over, the one named last changes fastest.
Arguments:
- tet_state: bfloat16 [175, 32768], P(None, ('axial', 'azim')), may hold values from -6 to 6
- prism_state: bfloat16 [375, 32768], P(None, ('axial', 'azim')), may hold values from -6 to 6
- tet_volume: bfloat16 [175, 175], replicated, may hold values from -0.4375 to 0.4375
- prism_volume: bfloat16 [375, 375], replicated, may hold values from -0.3125 to 0.3125
- face_extrap: bfloat16 [300, 175], replicated, may hold values from -0.4375 to 0.4375
- face_lift: bfloat16 [175, 300], replicated, may hold values from -0.75 to 0.75
- wall_extrap: bfloat16 [75, 375], replicated, may hold values from -0.3125 to 0.3125
- wall_lift: bfloat16 [375, 75], replicated, may hold values from -0.75 to 0.75
- face_code: int32 [32768], P(('axial', 'azim')), may hold values from 0 to 4095, as said below
- face_count: int32 [32, 2], P(('axial', 'azim')), may hold values from 0 to 512, as said below
- face_area: float32 [32768], P(('axial', 'azim')), may hold values from 0.5 to 2
- burn_prism: int32 [16384], P(('axial', 'azim')), may hold values from 0 to 1023, as said below
- burn_owner: int32 [16384, 1], P(('axial', 'azim')), may hold values from 0 to 3; in each aligned block of 512 rows (0 to 511, 512 to 1023, ...) at most 128 rows name the same one
- burn_law: float32 [8, 4, 6], P('axial'), may hold values from 0.5 to 2
Outputs:
- tet_new: bfloat16 [175, 32768], P(None, ('axial', 'azim'))
- prism_new: bfloat16 [375, 32768], P(None, ('axial', 'azim'))
Inputs may be any that keep to these rules, and one draw needn't show every extreme that they name: `face_code`: within each partition's block of 1024 entries the codes are distinct; the first 512 are faces shared with the lower axial neighbour, the rest with the upper; upper slot s of (a, z) is the same face as lower slot s of (a+1, z). `face_count`: column 0 counts live lower slots, column 1 live upper slots; the upper count of (a, z) equals the lower count of (a+1, z); zero at the two ends of the axial range, 1 or more elsewhere; 512 is reached. `burn_prism`: distinct within each partition's block. `burn_owner`: at most 128 wall faces of one partition name one owner, and that bound is reached.
All inputs are finite; a program needn't handle non-finite values.
Results may differ from a plain program's by a relative error of at most 0.0043.
Values may be sent and summed in bfloat16 or wider, within the bound.
A program may use at most 64 MiB of HBM per device.

v0:
```python
import jax
import jax.numpy as jnp
from jax import lax
from jax.sharding import PartitionSpec as P

NV = 5
TFP = 15
BW_DEV = 512
CB = 128


section_step = 0.25


def extended_2(block, sides, width):
    for axis, dim in sides:
        count = lax.axis_size(axis)
        forward = [(i, i + 1) for i in range(count - 1)]
        backward = [(target, source) for source, target in forward]
        low = lax.ppermute(
            lax.slice_in_dim(block, block.shape[dim] - width, None, axis=dim), axis, forward
        )
        high = lax.ppermute(lax.slice_in_dim(block, 0, width, axis=dim), axis, backward)
        block = jnp.concatenate([low, block, high], axis=dim)
    return block


def square_half(values):
    widened = values.astype(jnp.float32)
    return (0.5 * widened * widened).astype(jnp.bfloat16)


def on_device(
    tet_state,
    prism_state,
    tet_volume,
    prism_volume,
    face_extrap,
    face_lift,
    wall_extrap,
    wall_lift,
    face_code,
    face_count,
    face_area,
    burn_prism,
    burn_owner,
    burn_law,
):
    face_rows = wall_extrap.shape[0]
    slots = face_code.shape[0]
    capacity = slots // 2
    face_ids = jnp.arange(4, dtype=jnp.int32)
    tet_div = jnp.dot(tet_volume, square_half(tet_state), preferred_element_type=jnp.float32)
    tet_index = face_code // 4
    chosen = (face_code % 4)[None, :] == face_ids[:, None]
    columns = jnp.take(tet_state, tet_index, axis=1)
    extended = jnp.dot(face_extrap, columns, preferred_element_type=jnp.float32).reshape(
        4, face_rows, slots
    )
    left_rows = jnp.sum(
        jnp.where(chosen[:, None, :], extended, jnp.zeros_like(extended)), axis=0
    ).astype(jnp.bfloat16)
    left_grid = left_rows.reshape(face_rows, 2, capacity)
    received = extended_2(left_grid, (("axial", 1),), 1)
    right_rows = jnp.concatenate([received[:, 0:1, :], received[:, 3:4, :]], axis=1).reshape(
        face_rows, slots
    )
    normal = jnp.concatenate(
        [-jnp.ones((capacity,), jnp.float32), jnp.ones((capacity,), jnp.float32)]
    )
    slot_index = jnp.arange(capacity, dtype=jnp.int32)
    active = (slot_index[None, :] < face_count[0][:, None]).reshape(slots)
    left_wide = left_rows.astype(jnp.float32)
    right_wide = right_rows.astype(jnp.float32)
    speed = jnp.maximum(jnp.abs(left_wide), jnp.abs(right_wide))
    flux_jump = 0.25 * normal * (right_wide * right_wide - left_wide * left_wide) - 0.5 * speed * (
        right_wide - left_wide
    )
    jump_rows = (jnp.where(active, face_area, jnp.zeros_like(face_area)) * flux_jump).astype(
        jnp.bfloat16
    )
    placed = jnp.where(
        chosen[:, None, :], jump_rows[None, :, :], jnp.zeros((4, face_rows, slots), jnp.bfloat16)
    ).reshape(4 * face_rows, slots)
    tet_lift = jnp.dot(face_lift, placed, preferred_element_type=jnp.float32)
    tet_total = tet_div.at[:, tet_index].add(tet_lift)
    tet_new = (tet_state.astype(jnp.float32) - section_step * tet_total).astype(jnp.bfloat16)
    prism_div = jnp.dot(prism_volume, square_half(prism_state), preferred_element_type=jnp.float32)
    prism_columns = jnp.take(prism_state, burn_prism, axis=1)
    wall_rows = jnp.dot(wall_extrap, prism_columns, preferred_element_type=jnp.float32).astype(
        jnp.bfloat16
    )
    sectors = lax.axis_size("azim")
    owners = burn_owner[:, 0]
    owner_int = (owners[:, None] == jnp.arange(sectors, dtype=jnp.int32)[None, :]).astype(jnp.int32)
    law_table = burn_law[0]
    before = jnp.cumsum(owner_int, axis=0) - owner_int
    ranks = jnp.sum(before * owner_int, axis=1)
    position = owners * CB + ranks
    place_table = (position[:, None] == jnp.arange(sectors * CB, dtype=jnp.int32)[None, :]).astype(
        jnp.bfloat16
    )
    outgoing = jnp.dot(wall_rows, place_table, preferred_element_type=jnp.float32).astype(
        jnp.bfloat16
    )
    outgoing = outgoing.reshape(face_rows, sectors, CB)
    incoming = lax.all_to_all(outgoing, "azim", split_axis=1, concat_axis=1, tiled=True)
    sector = lax.axis_index("azim")
    own_law = lax.dynamic_index_in_dim(law_table, sector, 0, keepdims=False)
    burn_coef = own_law[0]
    inject = own_law[1:6]
    incoming_wide = incoming.reshape(NV, TFP, sectors, CB).astype(jnp.float32)
    received_squares = incoming_wide[4] * incoming_wide[4]
    patch_total = burn_coef * jnp.sum(received_squares)
    damping = 1.0 / (1.0 + patch_total / (BW_DEV * TFP))
    response = (
        inject[:, None, None, None] * (burn_coef * damping * received_squares)[None] - incoming_wide
    ).astype(jnp.bfloat16)
    returned = lax.all_to_all(
        response.reshape(face_rows, sectors, CB), "azim", split_axis=1, concat_axis=1, tiled=True
    )
    wall_jump = lax.dot_general(
        returned.reshape(face_rows, sectors * CB),
        place_table,
        (((1,), (1,)), ((), ())),
        preferred_element_type=jnp.float32,
    ).astype(jnp.bfloat16)
    prism_lift = jnp.dot(wall_lift, wall_jump, preferred_element_type=jnp.float32)
    prism_total = prism_div.at[:, burn_prism].add(prism_lift)
    prism_new = (prism_state.astype(jnp.float32) - section_step * prism_total).astype(jnp.bfloat16)
    return (tet_new, prism_new)


def solution(mesh):
    placed = (
        P(None, ("axial", "azim")),
        P(None, ("axial", "azim")),
        P(),
        P(),
        P(),
        P(),
        P(),
        P(),
        P(("axial", "azim")),
        P(("axial", "azim"), None),
        P(("axial", "azim")),
        P(("axial", "azim")),
        P(("axial", "azim"), None),
        P("axial", None, None),
    )
    return jax.shard_map(
        on_device,
        mesh=mesh,
        in_specs=placed,
        out_specs=(P(None, ("axial", "azim")), P(None, ("axial", "azim"))),
        check_vma=False,
    )
```

profile of v0, /device:TPU:11, one launch (start us, length us, event | category | flops | bytes accessed | tf_op | source)
XLA Modules:
  0.0 69.4 jit_solution(13000547216252904543)
XLA Ops:
  0.7 0.7 %compare_select_fusion.1 = s32[512]{0:T(512)S(1)} fusion(s32[512]{0:T(512)} %param.25), kind=kLoop, calls=%fused_computation.66 | loop fusion | flops 1536 | bytes 4096 | tf_op jit(solution)/shard_map/select_n | solution.py:129
  1.4 0.7 compare_and_fusion.1
  2.1 1.5 %copy.43 = bf16[375,1024]{0,1:T(8,128)(2,1)S(1)} copy(bf16[375,1024]{1,0:T(8,128)(2,1)} %param.15) | data formatting | bytes 1536000 | tf_op args[1]
  3.6 0.7 %fusion.36 = s32[4,4,128]{2,1,0:T(4,128)S(1)} fusion(s32[4,128]{1,0:T(4,128)} %bitcast.58), kind=kLoop, calls=%fused_computation.60 | loop fusion | flops 4096 | bytes 10240 | tf_op jit(solution)/shard_map/convert_element_type | solution.py:95
  4.3 1.2 %reduce-window.6 = s32[4,4,128]{2,1,0:T(4,128)S(1)} reduce-window(s32[4,4,128]{2,1,0:T(4,128)S(1)} %fusion.36, s32[]{:T(128)} %constant.57.clone.1), window={size=1x1x128 pad=0_0x0_0x127_0}, to_apply=%region_2.3 | reduce-window | flops 260096 | bytes 16388 | tf_op jit(solution)/shard_map/reduce-window
  5.5 0.2 slice_reduce_fusion
  5.7 0.2 reduce-window.9
  5.9 0.1 add_bitcast_fusion
  6.1 1.9 %gather_fusion.1 = bf16[512,375]{1,0:T(8,128)(2,1)S(1)} fusion(bf16[375,1024]{0,1:T(8,128)(2,1)S(1)} %copy.43, s32[1024]{0:T(1024)S(1)} %pad_clamp_fusion), kind=kCustom, calls=%fused_computation.1 | custom fusion | bytes 770048 | tf_op jit(solution)/shard_map/jit(_take)/gather | solution.py:89
  8.0 0.5 convolution_convert_fusion.2
  8.6 0.6 copy.45
  9.3 4.1 %all-to-all-start = ((bf16[75,4,128]{2,0,1:T(8,128)(2,1)}), bf16[75,4,128]{2,0,1:T(8,128)(2,1)S(1)}, u32[]{:S(2)}, u32[]{:S(2)}) async-start(bf16[75,4,128]{2,0,1:T(8,128)(2,1)} %copy.45), calls=%async_computation | async-start | bytes 163840 | tf_op jit(solution)/shard_map/all_to_all | solution.py:107
  13.4 0.2 copy.39
  13.6 3.9 %gather_fusion = bf16[1024,175]{1,0:T(8,128)(2,1)S(1)} fusion(bf16[175,1024]{0,1:T(8,128)(2,1)S(1)} %copy.39, s32[1024]{0:T(1024)S(1)} %broadcast_clamp_fusion), kind=kCustom, calls=%fused_computation | custom fusion | bytes 720896 | tf_op jit(solution)/shard_map/jit(_take)/gather | solution.py:56
  17.6 1.5 %convolution_bitcast_fusion.1 = f32[300,1024]{1,0:T(8,128)} fusion(bf16[300,175]{0,1:T(8,128)(2,1)S(1)} %copy-done.6, bf16[1024,175]{1,0:T(8,128)(2,1)S(1)} %gather_fusion, pred[1024]{0:T(1024)(128)(4,1)S(1)} %get-tuple-element.8), kind=kOutput, calls=%fused_computation.10 | convolution fusion | flops 107699200 | bytes 1693224 | tf_op jit(solution)/shard_map/dot_general | solution.py:57
  19.1 1.4 %reshape.143 = f32[4,75,1024]{2,1,0:T(8,128)S(1)} reshape(f32[300,1024]{1,0:T(8,128)} %convolution_bitcast_fusion.1) | data formatting | bytes 2457600 | tf_op jit(solution)/shard_map/reshape | solution.py:57
  20.6 0.1 select_reduce_fusion
  20.8 0.1 convert_element_type.85
  20.9 0.9 %fusion.44 = (bf16[75,1,512]{2,1,0:T(2,128)(2,1)}, bf16[75,1,512]{2,1,0:T(2,128)(2,1)}) fusion(bf16[75,2,512]{2,1,0:T(2,128)(2,1)S(1)} %convert_element_type.85), kind=kLoop, calls=%fused_computation.83 | loop fusion | bytes 307200 | tf_op jit(solution)/shard_map/slice | solution.py:21
  21.8 3.1 %collective-permute-start = (bf16[75,1,512]{2,1,0:T(2,128)(2,1)}, bf16[75,1,512]{2,1,0:T(2,128)(2,1)}, u32[]{:S(2)}, u32[]{:S(2)}) collective-permute-start(bf16[75,1,512]{2,1,0:T(2,128)(2,1)} %get-tuple-element.10), channel_id=1, source_target_pairs={{0,4},{4,8},{8,12},{12,16},{16,20},{20,24},{24,28},{1,5},{5,9},{9,... | collective-permute-start | bytes 230408 | tf_op jit(solution)/shard_map/ppermute | solution.py:20
  24.9 3.0 %collective-permute-start.1 = (bf16[75,1,512]{2,1,0:T(2,128)(2,1)}, bf16[75,1,512]{2,1,0:T(2,128)(2,1)}, u32[]{:S(2)}, u32[]{:S(2)}) collective-permute-start(bf16[75,1,512]{2,1,0:T(2,128)(2,1)} %get-tuple-element.11), channel_id=1, source_target_pairs={{4,0},{8,4},{12,8},{16,12},{20,16},{24,20},{28,24},{5,1},{9,5},{13... | collective-permute-start | bytes 230408 | tf_op jit(solution)/shard_map/ppermute | solution.py:23
  28.0 1.8 %convolution_bitcast_fusion = f32[375,1024]{1,0:T(8,128)} fusion(bf16[375,375]{1,0:T(8,128)(2,1)S(1)} %copy-done, bf16[375,1024]{0,1:T(8,128)(2,1)S(1)} %copy.43), kind=kOutput, calls=%fused_computation.9 | convolution fusion | flops 289536000 | bytes 2585250 | tf_op jit(solution)/shard_map/dot_general | solution.py:88
  29.8 0.1 iota_compare_fusion.7
  29.9 1.2 %convolution_bitcast_fusion.2 = f32[175,1024]{1,0:T(8,128)} fusion(bf16[175,175]{1,0:T(8,128)(2,1)S(1)} %copy-done.7, bf16[175,1024]{0,1:T(8,128)(2,1)S(1)} %copy.39), kind=kOutput, calls=%fused_computation.13 | convolution fusion | flops 63436800 | bytes 1136450 | tf_op jit(solution)/shard_map/dot_general | solution.py:53
  31.1 0.7 constant_dynamic-slice_fusion
  31.8 0.1 slice_bitcast_fusion
  31.9 0.1 mul.156
  31.9 0.1 mul.157
  32.0 1.9 %copy.50 = f32[375,1024]{0,1:T(8,128)S(1)} copy(f32[375,1024]{1,0:T(8,128)} %convolution_bitcast_fusion) | data formatting | bytes 3072000 | tf_op jit(solution)/shard_map/dot_general | solution.py:88
  33.9 1.4 %copy.41 = f32[175,1024]{0,1:T(8,128)S(1)} copy(f32[175,1024]{1,0:T(8,128)} %convolution_bitcast_fusion.2) | data formatting | bytes 1433600 | tf_op jit(solution)/shard_map/dot_general | solution.py:53
  35.4 0.6 fusion.32
  36.8 0.1 fusion.30
  36.9 0.7 copy.48
  37.6 3.9 %all-to-all-start.1 = ((bf16[75,4,128]{2,0,1:T(8,128)(2,1)}), bf16[75,4,128]{2,0,1:T(8,128)(2,1)S(1)}, u32[]{:S(2)}, u32[]{:S(2)}) async-start(bf16[75,4,128]{2,0,1:T(8,128)(2,1)} %copy.48), calls=%async_computation.1 | async-start | bytes 163840 | tf_op jit(solution)/shard_map/all_to_all | solution.py:119
  41.5 1.4 %maximum_convert_fusion = f32[75,2,512]{2,1,0:T(2,128)S(1)} fusion(bf16[75,1,512]{2,1,0:T(2,128)(2,1)} %collective-permute-done.1, bf16[75,1,512]{2,1,0:T(2,128)(2,1)} %collective-permute-done), kind=kLoop, calls=%fused_computation.43 | loop fusion | flops 307200 | bytes 460800 | tf_op jit(solution)/shard_map/convert_element_type | solution.py:74
  42.9 0.1 pad.4
  43.0 0.1 copy.56
  43.1 0.1 fusion.22
  43.2 0.9 %broadcast_select_fusion = bf16[4,75,1024]{2,1,0:T(8,128)(2,1)} fusion(pred[4,1024]{1,0:T(4,128)(4,1)S(1)} %iota_compare_fusion.4, bf16[75,1024]{1,0:T(8,128)(2,1)S(1)} %fusion.22), kind=kLoop, calls=%fused_computation.22 | loop fusion | flops 307200 | bytes 772096 | tf_op jit(solution)/shard_map/jit(_where)/select_n | solution.py:82
  44.1 2.1 %select_n.58 = bf16[300,1024]{1,0:T(8,128)(2,1)} reshape(bf16[4,75,1024]{2,1,0:T(8,128)(2,1)} %broadcast_select_fusion) | data formatting | bytes 1228800 | tf_op jit(solution)/shard_map/jit(_where)/select_n | solution.py:82
  46.2 2.6 %fusion.45 = f32[1024,175]{1,0:T(8,128)} fusion(bf16[300,1024]{1,0:T(8,128)(2,1)} %select_n.58, bf16[175,300]{1,0:T(8,128)(2,1)} %param.19), kind=kOutput, calls=%fused_computation.84 | convolution fusion | flops 107520000 | bytes 1436200 | tf_op jit(solution)/shard_map/dot_general | solution.py:85
  48.8 6.9 %scatter_fusion = f32[175,1024]{0,1:T(8,128)S(1)} fusion(f32[175,1024]{0,1:T(8,128)S(1)} %copy.41, s32[1024]{0:T(1024)S(1)} %get-tuple-element.9, f32[1024,175]{1,0:T(8,128)} %fusion.45), kind=kCustom, calls=%fused_computation.2 | custom fusion | flops 179200 | bytes 2154496 | tf_op jit(solution)/shard_map/scatter-add | solution.py:86
  55.7 0.9 %fusion.3 = bf16[175,1024]{0,1:T(8,128)(2,1)} fusion(bf16[175,1024]{0,1:T(8,128)(2,1)S(1)} %copy.39, f32[175,1024]{0,1:T(8,128)S(1)} %scatter_fusion), kind=kLoop, calls=%fused_computation.18 | loop fusion | flops 716800 | bytes 1433600 | tf_op jit(solution)/shard_map/convert_element_type | solution.py:87
  56.6 2.0 %copy.52 = bf16[175,1024]{1,0:T(8,128)(2,1)} copy(bf16[175,1024]{0,1:T(8,128)(2,1)} %fusion.3) | data formatting | bytes 716800
  58.7 2.4 %fusion.2 = f32[512,375]{1,0:T(8,128)} fusion(bf16[375,75]{0,1:T(8,128)(2,1)} %param.21, bf16[75,512]{1,0:T(8,128)(2,1)S(1)} %bitcast.56, s32[512]{0:T(512)S(1)} %bitcast.61), kind=kOutput, calls=%fused_computation.17 | convolution fusion | flops 68422144 | bytes 903098 | tf_op jit(solution)/shard_map/dot_general | solution.py:128
  61.1 4.9 %scatter_fusion.1 = f32[375,1024]{0,1:T(8,128)S(1)} fusion(f32[375,1024]{0,1:T(8,128)S(1)} %copy.50, s32[512]{0:T(512)S(1)} %compare_select_fusion.1, f32[512,375]{1,0:T(8,128)} %fusion.2), kind=kCustom, calls=%fused_computation.3 | custom fusion | flops 192000 | bytes 2306048 | tf_op jit(solution)/shard_map/scatter-add | solution.py:129
  66.1 1.1 %fusion = bf16[375,1024]{0,1:T(8,128)(2,1)} fusion(bf16[375,1024]{0,1:T(8,128)(2,1)S(1)} %copy-done.2, f32[375,1024]{0,1:T(8,128)S(1)} %scatter_fusion.1), kind=kLoop, calls=%fused_computation.6 | loop fusion | flops 1536000 | bytes 3072000 | tf_op jit(solution)/shard_map/convert_element_type | solution.py:130
  67.1 2.3 %copy.53 = bf16[375,1024]{1,0:T(8,128)(2,1)} copy(bf16[375,1024]{0,1:T(8,128)(2,1)} %fusion) | data formatting | bytes 1536000
  (47 shorter events, 0.4 us)
Async XLA Ops:
  0.6 27.4 %copy-start = (bf16[375,375]{1,0:T(8,128)(2,1)S(1)}, bf16[375,375]{1,0:T(8,128)(2,1)}, u32[]{:S(2)}) copy-start(bf16[375,375]{1,0:T(8,128)(2,1)} %param.17) | copy-start | bytes 843754
  0.6 5.4 %copy-start.8 = (s32[512,1]{0,1:T(1,128)S(1)}, s32[512,1]{0,1:T(1,128)}, u32[]{:S(2)}) copy-start(s32[512,1]{0,1:T(1,128)} %param.26) | copy-start | bytes 6148
  3.6 24.4 %copy-start.1 = (bf16[375,1024]{0,1:T(8,128)(2,1)}, bf16[375,1024]{0,1:T(8,128)(2,1)S(1)}, u32[]{:S(2)}) copy-start(bf16[375,1024]{0,1:T(8,128)(2,1)S(1)} %copy.43) | copy-start | bytes 2304004
  6.0 2.0 %copy-start.13 = (bf16[75,375]{1,0:T(8,128)(2,1)S(1)}, bf16[75,375]{1,0:T(8,128)(2,1)}, u32[]{:S(2)}) copy-start(bf16[75,375]{1,0:T(8,128)(2,1)} %param.20) | copy-start | bytes 168754
  8.0 5.4 %copy-start.9 = (s32[1024]{0:T(1024)S(1)}, s32[1024]{0:T(1024)}, u32[]{:S(2)}) copy-start(s32[1024]{0:T(1024)} %param.22) | copy-start | bytes 12292
  8.0 5.4 %copy-start.5 = (bf16[175,1024]{1,0:T(8,128)(2,1)S(1)}, bf16[175,1024]{1,0:T(8,128)(2,1)}, u32[]{:S(2)}) copy-start(bf16[175,1024]{1,0:T(8,128)(2,1)} %param.14) | copy-start | bytes 1075204
  9.3 26.1 %all-to-all-start = ((bf16[75,4,128]{2,0,1:T(8,128)(2,1)}), bf16[75,4,128]{2,0,1:T(8,128)(2,1)S(1)}, u32[]{:S(2)}, u32[]{:S(2)}) async-start(bf16[75,4,128]{2,0,1:T(8,128)(2,1)} %copy.45), calls=%async_computation | async-start | bytes 163840 | tf_op jit(solution)/shard_map/all_to_all | solution.py:107
  13.6 4.0 %copy-start.6 = (bf16[300,175]{0,1:T(8,128)(2,1)S(1)}, bf16[300,175]{0,1:T(8,128)(2,1)}, u32[]{:S(2)}) copy-start(bf16[300,175]{0,1:T(8,128)(2,1)} %param.18) | copy-start | bytes 315004
  20.8 9.1 %copy-start.3 = (bf16[75,1024]{1,0:T(8,128)(2,1)}, bf16[75,1024]{1,0:T(8,128)(2,1)S(1)}, u32[]{:S(2)}) copy-start(bf16[75,1024]{1,0:T(8,128)(2,1)S(1)} %select_reduce_fusion) | copy-start | bytes 460804
  20.9 9.0 %copy-start.12 = (s32[1,2]{1,0:T(1,128)S(1)}, s32[1,2]{1,0:T(1,128)}, u32[]{:S(2)}) copy-start(s32[1,2]{1,0:T(1,128)} %param.23) | copy-start | bytes 28
  20.9 9.0 %copy-start.7 = (bf16[175,175]{1,0:T(8,128)(2,1)S(1)}, bf16[175,175]{1,0:T(8,128)(2,1)}, u32[]{:S(2)}) copy-start(bf16[175,175]{1,0:T(8,128)(2,1)} %param.16) | copy-start | bytes 183754
  21.8 19.7 %collective-permute-start = (bf16[75,1,512]{2,1,0:T(2,128)(2,1)}, bf16[75,1,512]{2,1,0:T(2,128)(2,1)}, u32[]{:S(2)}, u32[]{:S(2)}) collective-permute-start(bf16[75,1,512]{2,1,0:T(2,128)(2,1)} %get-tuple-element.10), channel_id=1, source_target_pairs={{0,4},{4,8},{8,12},{12,16},{16,20},{20,24},{24,28},{1,5},{5,9},{9,... | collective-permute-start | bytes 230408 | tf_op jit(solution)/shard_map/ppermute | solution.py:20
  24.9 16.5 %collective-permute-start.1 = (bf16[75,1,512]{2,1,0:T(2,128)(2,1)}, bf16[75,1,512]{2,1,0:T(2,128)(2,1)}, u32[]{:S(2)}, u32[]{:S(2)}) collective-permute-start(bf16[75,1,512]{2,1,0:T(2,128)(2,1)} %get-tuple-element.11), channel_id=1, source_target_pairs={{4,0},{8,4},{12,8},{16,12},{20,16},{24,20},{28,24},{5,1},{9,5},{13... | collective-permute-start | bytes 230408 | tf_op jit(solution)/shard_map/ppermute | solution.py:23
  28.0 3.8 %copy-start.10 = (f32[1024]{0:T(1024)S(1)}, f32[1024]{0:T(1024)}, u32[]{:S(2)}) copy-start(f32[1024]{0:T(1024)} %param.24) | copy-start | bytes 12292
  35.3 7.7 %copy-start.11 = (f32[1024]{0:T(1024)S(1)}, f32[1024]{0:T(1024)}, u32[]{:S(2)}) copy-start(f32[1024]{0:T(1024)} %constant.87.clone.1) | copy-start | bytes 12292
  37.6 21.0 %all-to-all-start.1 = ((bf16[75,4,128]{2,0,1:T(8,128)(2,1)}), bf16[75,4,128]{2,0,1:T(8,128)(2,1)S(1)}, u32[]{:S(2)}, u32[]{:S(2)}) async-start(bf16[75,4,128]{2,0,1:T(8,128)(2,1)} %copy.48), calls=%async_computation.1 | async-start | bytes 163840 | tf_op jit(solution)/shard_map/all_to_all | solution.py:119
  41.5 1.6 %copy-start.4 = (bf16[75,1024]{1,0:T(8,128)(2,1)S(1)}, bf16[75,1024]{1,0:T(8,128)(2,1)}, u32[]{:S(2)}) copy-start(bf16[75,1024]{1,0:T(8,128)(2,1)} %copy-done.3) | copy-start | bytes 460804
  61.1 4.9 %copy-start.2 = (bf16[375,1024]{0,1:T(8,128)(2,1)S(1)}, bf16[375,1024]{0,1:T(8,128)(2,1)}, u32[]{:S(2)}) copy-start(bf16[375,1024]{0,1:T(8,128)(2,1)} %copy-done.1) | copy-start | bytes 2304004
where the time goes:
time: 70.3 us; the launch traced here: 69.4 us
  local copies, waits for them, and re-layouts  22.5 us (32%)
  other arithmetic  21 us (30%)
  starting transfers between devices  14.2 us (20%)
  matrix products  9.99 us (14%)
  between operations  1.79 us (3%)
    scatter-add x1, other arithmetic, on_device(): tet_total = tet_div.at[:, tet_index].add(tet_lift)  6.93 us
    unnamed x36, local copies, waits for them, and re-layouts  6.23 us
    scatter-add x1, other arithmetic, on_device(): prism_total = prism_div.at[:, burn_prism].add(prism_lift)  4.93 us
    all_to_all x1, starting transfers between devices, on_device(): lax.all_to_all(outgoing, 'azim', split_axis=1, concat_axis=1, tiled=True)  4.11 us
    gather x1, local copies, waits for them, and re-layouts, on_device(): columns = jnp.take(tet_state, tet_index, axis=1)  3.94 us
    all_to_all x1, starting transfers between devices, on_device(): lax.all_to_all(response.reshape(face_rows, sectors, CB), 'azim', split_ax...  3.87 us
    ppermute x1, starting transfers between devices, extended_2(): lax.ppermute(lax.slice_in_dim(block, block.shape[dim] - width, None, axis...  3.14 us
    ppermute x1, starting transfers between devices, extended_2(): lax.ppermute(lax.slice_in_dim(block, 0, width, axis=dim), axis, backward)  3.04 us
  transfers between devices with their start and end apart: 4, of which 0 were waited for; matrix products, arithmetic and copies ran while one was open for 49% of the time, Pallas kernels for 0%

commit v1 on v0

v1 whole, which is shorter than its diff:
```python
import functools

import jax
import jax.numpy as jnp
from jax import lax
from jax.experimental import pallas as pl
from jax.experimental.pallas import tpu as pltpu
from jax.sharding import PartitionSpec as P

NV = 5
TFP = 15
FACES = 4
FACE_PAD = 80
VAR_PAD = 16
OWNER_ROWS = 8
CHUNK = 256

section_step = 0.25
F32 = jnp.float32
BF16 = jnp.bfloat16


def dot(left, right):
    return jnp.dot(left, right, preferred_element_type=F32)


def dot_t(left, right):
    return lax.dot_general(left, right, (((1,), (1,)), ((), ())), preferred_element_type=F32)


def square_half(values):
    widened = values.astype(F32)
    return (0.5 * widened * widened).astype(BF16)


def spread(groups, width, padded):
    row = lax.broadcasted_iota(jnp.int32, (groups * padded, groups * width), 0)
    column = lax.broadcasted_iota(jnp.int32, (groups * padded, groups * width), 1)
    group = jnp.zeros_like(row)
    for g in range(1, groups):
        group = group + (row >= g * padded).astype(jnp.int32)
    hit = (column == row - group * (padded - width)) & (row - group * padded < width)
    return jnp.where(hit, 1.0, 0.0).astype(BF16)


def one_hot(index, base, rows):
    row = lax.broadcasted_iota(jnp.int32, (rows, index.shape[1]), 0) + base
    return jnp.where(row == index, 1.0, 0.0).astype(BF16)


def kernel(
    n_axial,
    n_azim,
    tet_ref,
    prism_ref,
    tet_volume,
    prism_volume,
    face_extrap,
    face_lift,
    wall_extrap,
    wall_lift,
    code_ref,
    area_ref,
    burn_ref,
    owner_ref,
    count_ref,
    law_ref,
    tet_out,
    prism_out,
    hot,
    send,
    recv,
    div,
    part,
    parts,
    send_sem,
    recv_sem,
    part_send_sem,
    part_recv_sem,
):
    axial = lax.axis_index("axial")
    azim = lax.axis_index("azim")
    has_low = axial > 0
    has_high = axial < n_axial - 1
    low = (jnp.maximum(axial - 1, 0), azim)
    high = (jnp.minimum(axial + 1, n_axial - 1), azim)
    others = [(axial, lax.rem(azim + d, n_azim)) for d in range(1, n_azim)]
    mesh_id = pl.DeviceIdType.MESH

    barrier = pltpu.get_barrier_semaphore()

    @pl.when(has_low)
    def _():
        pl.semaphore_signal(barrier, inc=1, device_id=low, device_id_type=mesh_id)

    @pl.when(has_high)
    def _():
        pl.semaphore_signal(barrier, inc=1, device_id=high, device_id_type=mesh_id)

    for other in others:
        pl.semaphore_signal(barrier, inc=1, device_id=other, device_id_type=mesh_id)

    tets = tet_ref.shape[1]
    prisms = prism_ref.shape[1]
    slots = code_ref.shape[1]
    half = slots // 2

    code = code_ref[...]
    tet_index = code // FACES
    face = code - FACES * tet_index
    tet_state = tet_ref[...]
    faces_spread = spread(FACES, face_extrap.shape[0] // FACES, FACE_PAD)
    extrap = dot(faces_spread, face_extrap[...]).astype(BF16)
    lift = dot_t(face_lift[...], faces_spread).astype(BF16)
    for first in range(0, slots, CHUNK):
        lanes = slice(first, first + CHUNK)
        for base in range(0, tets, CHUNK):
            hot[base : base + CHUNK, lanes] = one_hot(tet_index[:, lanes], base, CHUNK)
        columns = dot(tet_state, hot[:, lanes]).astype(BF16)
        extended = dot(extrap, columns)
        rows = extended[0:FACE_PAD]
        for f in range(1, FACES):
            rows = jnp.where(
                face[:, lanes] == f, extended[f * FACE_PAD : (f + 1) * FACE_PAD], rows
            )
        side, offset = first // half, first % half
        send[side, :, offset : offset + CHUNK] = rows.astype(BF16)

    @pl.when(has_low & has_high)
    def _():
        pl.semaphore_wait(barrier, n_azim + 1)

    @pl.when(jnp.logical_not(has_low & has_high))
    def _():
        pl.semaphore_wait(barrier, n_azim)

    def face_copy(side, device):
        return pltpu.make_async_remote_copy(
            src_ref=send.at[side],
            dst_ref=recv.at[1 - side],
            send_sem=send_sem.at[side],
            recv_sem=recv_sem.at[1 - side],
            device_id=device,
            device_id_type=mesh_id,
        )

    @pl.when(has_low)
    def _():
        face_copy(0, low).start()

    @pl.when(has_high)
    def _():
        face_copy(1, high).start()

    wall_spread = spread(NV, TFP, VAR_PAD)
    wall_out = dot(wall_spread, wall_extrap[...]).astype(BF16)
    wall_in = dot_t(wall_lift[...], wall_spread).astype(BF16)
    prism_state = prism_ref[...]
    wall_rows = dot(wall_out, prism_state).astype(BF16).astype(F32)
    squares = wall_rows[(NV - 1) * VAR_PAD : NV * VAR_PAD]
    squares = squares * squares
    owner_row = lax.broadcasted_iota(jnp.int32, (OWNER_ROWS, owner_ref.shape[1]), 0)
    owner_hot = jnp.where(owner_row == owner_ref[...], 1.0, 0.0).astype(BF16)
    owned = dot_t(owner_hot, one_hot(burn_ref[...], 0, prisms))
    partial = jnp.sum(owned * jnp.sum(squares, axis=0, keepdims=True), axis=1, keepdims=True)
    part[...] = jnp.broadcast_to(partial, part.shape)

    def part_copy(source, d):
        return pltpu.make_async_remote_copy(
            src_ref=part,
            dst_ref=parts.at[source],
            send_sem=part_send_sem.at[d],
            recv_sem=part_recv_sem.at[source],
            device_id=others[d],
            device_id_type=mesh_id,
        )

    for d in range(n_azim - 1):
        part_copy(azim, d).start()

    div[...] = dot(prism_volume[...], square_half(prism_state))
    tet_flux = square_half(tet_state)

    @pl.when(has_low)
    def _():
        face_copy(0, low).wait_send()
        face_copy(1, low).wait_recv()

    @pl.when(jnp.logical_not(has_low))
    def _():
        recv[0] = jnp.zeros(recv.shape[1:], BF16)

    @pl.when(has_high)
    def _():
        face_copy(1, high).wait_send()
        face_copy(0, high).wait_recv()

    @pl.when(jnp.logical_not(has_high))
    def _():
        recv[1] = jnp.zeros(recv.shape[1:], BF16)

    slot = lax.broadcasted_iota(jnp.int32, (1, half), 1)
    jumps = []
    for side in range(2):
        lanes = slice(side * half, (side + 1) * half)
        left = send[side].astype(F32)
        right = recv[side].astype(F32)
        speed = jnp.maximum(jnp.abs(left), jnp.abs(right))
        step = right - left
        normal = 0.25 if side else -0.25
        flux_jump = normal * (right * right - left * left) - 0.5 * speed * step
        area = jnp.where(slot < count_ref[0, side], area_ref[:, lanes], 0.0)
        jumps.append((area * flux_jump).astype(BF16))
    jump = jnp.concatenate(jumps, axis=1)
    zero = jnp.zeros_like(jump)
    placed = jnp.concatenate([jnp.where(face == f, jump, zero) for f in range(FACES)], axis=0)
    for first in range(0, tets, CHUNK):
        lanes = slice(first, first + CHUNK)
        on_tets = dot_t(placed, hot[lanes, :]).astype(BF16)
        total = dot(tet_volume[...], tet_flux[:, lanes]) + dot(lift, on_tets)
        tet_out[:, lanes] = (tet_state[:, lanes].astype(F32) - section_step * total).astype(BF16)

    sums = part[...]
    for d in range(n_azim - 1):
        part_copy(azim, d).wait_send()
        source = others[d][1]
        part_copy(source, d).wait_recv()
        sums = sums + parts[source]
    faces = owner_ref.shape[1]
    inject = [jnp.zeros((1, prisms), F32) for _ in range(NV)]
    walls = jnp.zeros((1, prisms), F32)
    for o in range(n_azim):
        burn = law_ref[o, 0]
        damping = 1.0 / (1.0 + burn * sums[o : o + 1, 0:1] / (faces * TFP))
        scale = owned[o : o + 1] * (burn * damping)
        walls = walls + owned[o : o + 1]
        for v in range(NV):
            inject[v] = inject[v] + law_ref[o, 1 + v] * scale
    wall_jump = jnp.concatenate(
        [
            jnp.where(
                walls > 0.5,
                inject[v] * squares - wall_rows[v * VAR_PAD : (v + 1) * VAR_PAD],
                0.0,
            )
            for v in range(NV)
        ],
        axis=0,
    ).astype(BF16)
    for first in range(0, prisms, CHUNK):
        lanes = slice(first, first + CHUNK)
        total = div[:, lanes] + dot(wall_in, wall_jump[:, lanes])
        prism_out[:, lanes] = (
            prism_state[:, lanes].astype(F32) - section_step * total
        ).astype(BF16)


def on_device(
    n_axial,
    n_azim,
    tet_state,
    prism_state,
    tet_volume,
    prism_volume,
    face_extrap,
    face_lift,
    wall_extrap,
    wall_lift,
    face_code,
    face_count,
    face_area,
    burn_prism,
    burn_owner,
    burn_law,
):
    slots = face_code.shape[0]
    faces = burn_prism.shape[0]
    vmem = pl.BlockSpec(memory_space=pltpu.VMEM)
    smem = pl.BlockSpec(memory_space=pltpu.SMEM)
    return pl.pallas_call(
        functools.partial(kernel, n_axial, n_azim),
        out_shape=(
            jax.ShapeDtypeStruct(tet_state.shape, BF16),
            jax.ShapeDtypeStruct(prism_state.shape, BF16),
        ),
        in_specs=[vmem] * 12 + [smem] * 2,
        out_specs=(vmem, vmem),
        scratch_shapes=[
            pltpu.VMEM((tet_state.shape[1], slots), BF16),
            pltpu.VMEM((2, FACE_PAD, slots // 2), BF16),
            pltpu.VMEM((2, FACE_PAD, slots // 2), BF16),
            pltpu.VMEM(prism_state.shape, F32),
            pltpu.VMEM((OWNER_ROWS, 128), F32),
            pltpu.VMEM((n_azim, OWNER_ROWS, 128), F32),
            pltpu.SemaphoreType.DMA((2,)),
            pltpu.SemaphoreType.DMA((2,)),
            pltpu.SemaphoreType.DMA((n_azim - 1,)),
            pltpu.SemaphoreType.DMA((n_azim,)),
        ],
        compiler_params=pltpu.CompilerParams(
            collective_id=0, has_side_effects=True, vmem_limit_bytes=48 * 1024 * 1024
        ),
    )(
        tet_state,
        prism_state,
        tet_volume,
        prism_volume,
        face_extrap,
        face_lift,
        wall_extrap,
        wall_lift,
        face_code.reshape(1, slots),
        face_area.reshape(1, slots),
        burn_prism.reshape(1, faces),
        burn_owner.reshape(1, faces),
        face_count,
        burn_law[0],
    )


def solution(mesh):
    placed = (
        P(None, ("axial", "azim")),
        P(None, ("axial", "azim")),
        P(),
        P(),
        P(),
        P(),
        P(),
        P(),
        P(("axial", "azim")),
        P(("axial", "azim"), None),
        P(("axial", "azim")),
        P(("axial", "azim")),
        P(("axial", "azim"), None),
        P("axial", None, None),
    )
    return jax.shard_map(
        functools.partial(on_device, mesh.shape["axial"], mesh.shape["azim"]),
        mesh=mesh,
        in_specs=placed,
        out_specs=(P(None, ("axial", "azim")), P(None, ("axial", "azim"))),
        check_vma=False,
    )
```

time: 70.3 us -> 22.1 us (0.31)
  other arithmetic: 21 us -> 0 us
  starting transfers between devices: 14.2 us -> 0 us
  local copies, waits for them, and re-layouts: 22.5 us -> 9.57 us
  Pallas kernels: 0 us -> 11.4 us
  matrix products: 9.99 us -> 0 us
  between operations: 1.79 us -> 0.74 us
    scatter-add x2 -> x0, other arithmetic: 11.9 us -> none  [the longest x1 6.93 us: on_device(): tet_total = tet_div.at[:, tet_index].add(tet_lift)]
    pallas_call x0 -> x1, Pallas kernels: none -> 11.4 us  [on_device(): pl.pallas_call(functools.partial(kernel, n_axial, n_azim), out_shape=(jax...]
    dot_general x6 -> x0, matrix products: 9.99 us -> none  [the longest x1 2.56 us: on_device(): tet_lift = jnp.dot(face_lift, placed, preferred_element_type=jnp.float32)]
    all_to_all x2 -> x0, starting transfers between devices: 7.99 us -> none  [the longest x1 4.11 us: on_device(): lax.all_to_all(outgoing, 'azim', split_axis=1, concat_axis=1, tiled=True)]
    ppermute x2 -> x0, starting transfers between devices: 6.17 us -> none  [the longest x1 3.14 us: extended_2(): lax.ppermute(lax.slice_in_dim(block, block.shape[dim] - width, None, axis...]
    gather x2 -> x0, local copies, waits for them, and re-layouts: 5.88 us -> none  [the longest x1 3.94 us: on_device(): columns = jnp.take(tet_state, tet_index, axis=1)]
    convert_element_type x6 -> x0, other arithmetic: 4.43 us -> none  [the longest x1 1.38 us: on_device(): right_wide = right_rows.astype(jnp.float32)]
    unnamed x36 -> x28, local copies, waits for them, and re-layouts: 6.23 us -> 9.57 us
  transfers between devices with their start and end apart: 4 -> 0, of which waited for: 0 -> 0; matrix products, arithmetic and copies ran while one was open for 49% -> 0% of each run, Pallas kernels for 0% -> 0%
where the time goes in v1:
time: 22.1 us; the launch traced here: 21.7 us
  Pallas kernels  11.4 us (52%)
  local copies, waits for them, and re-layouts  9.57 us (43%)
  between operations  0.74 us (3%)
    pallas_call x1, Pallas kernels, on_device(): pl.pallas_call(functools.partial(kernel, n_axial, n_azim), out_shape=(jax...  11.4 us
    unnamed x28, local copies, waits for them, and re-layouts  9.57 us

profile of v1, /device:TPU:11, one launch (start us, length us, event | category | flops | bytes accessed | tf_op | source)
XLA Modules:
  0.0 21.7 jit_solution(2316244240717439348)
XLA Ops:
  0.6 0.0 copy-start.1
  0.6 1.0 %copy.17.wall_lift = bf16[375,75]{1,0:T(8,128)(2,1)S(1)} copy(bf16[375,75]{0,1:T(8,128)(2,1)} %param.21) | data formatting | bytes 112500 | tf_op args[7]
  1.6 0.0 copy-start.4
  1.7 0.0 copy-start.6
  1.7 0.0 copy-start.8
  1.7 0.0 copy-start.11
  1.7 1.1 %copy.16.face_extrap = bf16[300,175]{1,0:T(8,128)(2,1)S(1)} copy(bf16[300,175]{0,1:T(8,128)(2,1)} %param.18) | data formatting | bytes 210000 | tf_op args[4]
  2.8 0.0 copy-done.1
  2.8 0.0 copy-done.4
  2.8 0.0 copy-done.6
  2.8 0.0 copy-done.8
  2.8 0.0 copy-done.11
  2.8 0.0 copy-start
  2.8 1.1 %copy-done = bf16[375,1024]{1,0:T(8,128)(2,1)S(1)} copy-done((bf16[375,1024]{1,0:T(8,128)(2,1)S(1)}, bf16[375,1024]{1,0:T(8,128)(2,1)}, u32[]{:S(2)}) %copy-start) | copy-done | bytes 768024
  3.9 0.0 copy-start.2
  3.9 1.0 %copy-done.2 = bf16[375,375]{1,0:T(8,128)(2,1)S(1)} copy-done((bf16[375,375]{1,0:T(8,128)(2,1)S(1)}, bf16[375,375]{1,0:T(8,128)(2,1)}, u32[]{:S(2)}) %copy-start.2) | copy-done | bytes 281274
  4.9 0.0 copy-start.3
  4.9 0.9 %copy-done.3 = bf16[175,300]{1,0:T(8,128)(2,1)S(1)} copy-done((bf16[175,300]{1,0:T(8,128)(2,1)S(1)}, bf16[175,300]{1,0:T(8,128)(2,1)}, u32[]{:S(2)}) %copy-start.3) | copy-done | bytes 105024
  5.8 0.0 copy-start.5
  5.8 0.8 %copy-done.5 = bf16[75,375]{1,0:T(8,128)(2,1)S(1)} copy-done((bf16[75,375]{1,0:T(8,128)(2,1)S(1)}, bf16[75,375]{1,0:T(8,128)(2,1)}, u32[]{:S(2)}) %copy-start.5) | copy-done | bytes 56274
  6.6 0.0 copy-start.7
  6.6 0.7 %copy-done.7 = f32[1024]{0:T(1024)S(1)} copy-done((f32[1024]{0:T(1024)S(1)}, f32[1024]{0:T(1024)}, u32[]{:S(2)}) %copy-start.7) | copy-done | bytes 4120
  7.3 0.0 copy-start.9
  7.3 0.7 %copy-done.9 = s32[512,1]{0,1:T(1,128)S(1)} copy-done((s32[512,1]{0,1:T(1,128)S(1)}, s32[512,1]{0,1:T(1,128)}, u32[]{:S(2)}) %copy-start.9) | copy-done | bytes 2072
  8.0 0.0 copy-start.10
  8.0 0.7 %copy-done.10 = f32[1,4,6]{2,1,0:T(4,128)S(1)} copy-done((f32[1,4,6]{2,1,0:T(4,128)S(1)}, f32[1,4,6]{2,1,0:T(4,128)}, u32[]{:S(2)}) %copy-start.10) | copy-done | bytes 120
  8.7 11.4 %shard_map.149 = (bf16[175,1024]{1,0:T(8,128)(2,1)S(1)}, bf16[375,1024]{1,0:T(8,128)(2,1)S(1)}) custom-call(bf16[175,1024]{1,0:T(8,128)(2,1)S(1)} %copy-done.1, bf16[375,1024]{1,0:T(8,128)(2,1)S(1)} %copy-done, bf16[175,175]{1,0:T(8,128)(2,1)S(1)} %copy-done.4, bf16[375,375]{1,0:T(8,128)(2,1)S(1)} %copy-done.2, bf16[300,175]{1,0:T(8,128)(2,1)S(1)} %copy.16.face_extrap, ...), custom_call_target="tpu_custom_call" | custom-call | tf_op jit(solution)/shard_map/pallas_call | solution.py:280
  20.1 0.7 %copy.20 = bf16[175,1024]{1,0:T(8,128)(2,1)} copy(bf16[175,1024]{1,0:T(8,128)(2,1)S(1)} %get-tuple-element.4) | data formatting | bytes 716800
  20.9 0.9 %copy.21 = bf16[375,1024]{1,0:T(8,128)(2,1)} copy(bf16[375,1024]{1,0:T(8,128)(2,1)S(1)} %get-tuple-element.5) | data formatting | bytes 1536000
Async XLA Ops:
  0.6 2.1 %copy-start.1 = (bf16[175,1024]{1,0:T(8,128)(2,1)S(1)}, bf16[175,1024]{1,0:T(8,128)(2,1)}, u32[]{:S(2)}) copy-start(bf16[175,1024]{1,0:T(8,128)(2,1)} %tet_ref.1) | copy-start | bytes 1075204
  1.6 1.1 %copy-start.4 = (bf16[175,175]{1,0:T(8,128)(2,1)S(1)}, bf16[175,175]{1,0:T(8,128)(2,1)}, u32[]{:S(2)}) copy-start(bf16[175,175]{1,0:T(8,128)(2,1)} %tet_volume.1) | copy-start | bytes 183754
  1.7 1.1 %copy-start.6 = (s32[1024]{0:T(1024)S(1)}, s32[1024]{0:T(1024)}, u32[]{:S(2)}) copy-start(s32[1024]{0:T(1024)} %param.22) | copy-start | bytes 12292
  1.7 1.1 %copy-start.8 = (s32[512]{0:T(512)S(1)}, s32[512]{0:T(512)}, u32[]{:S(2)}) copy-start(s32[512]{0:T(512)} %param.25) | copy-start | bytes 6148
  1.7 1.1 %copy-start.11 = (s32[1,2]{1,0:T(1,128)S(1)}, s32[1,2]{1,0:T(1,128)}, u32[]{:S(2)}) copy-start(s32[1,2]{1,0:T(1,128)} %count_ref.1) | copy-start | bytes 28
  2.8 1.1 %copy-start = (bf16[375,1024]{1,0:T(8,128)(2,1)S(1)}, bf16[375,1024]{1,0:T(8,128)(2,1)}, u32[]{:S(2)}) copy-start(bf16[375,1024]{1,0:T(8,128)(2,1)} %prism_ref.1) | copy-start | bytes 2304004
  3.9 1.0 %copy-start.2 = (bf16[375,375]{1,0:T(8,128)(2,1)S(1)}, bf16[375,375]{1,0:T(8,128)(2,1)}, u32[]{:S(2)}) copy-start(bf16[375,375]{1,0:T(8,128)(2,1)} %prism_volume.1) | copy-start | bytes 843754
  4.9 0.9 %copy-start.3 = (bf16[175,300]{1,0:T(8,128)(2,1)S(1)}, bf16[175,300]{1,0:T(8,128)(2,1)}, u32[]{:S(2)}) copy-start(bf16[175,300]{1,0:T(8,128)(2,1)} %face_lift.1) | copy-start | bytes 315004
  5.8 0.8 %copy-start.5 = (bf16[75,375]{1,0:T(8,128)(2,1)S(1)}, bf16[75,375]{1,0:T(8,128)(2,1)}, u32[]{:S(2)}) copy-start(bf16[75,375]{1,0:T(8,128)(2,1)} %wall_extrap.1) | copy-start | bytes 168754
  6.6 0.7 %copy-start.7 = (f32[1024]{0:T(1024)S(1)}, f32[1024]{0:T(1024)}, u32[]{:S(2)}) copy-start(f32[1024]{0:T(1024)} %param.24) | copy-start | bytes 12292
  7.3 0.7 %copy-start.9 = (s32[512,1]{0,1:T(1,128)S(1)}, s32[512,1]{0,1:T(1,128)}, u32[]{:S(2)}) copy-start(s32[512,1]{0,1:T(1,128)} %param.26) | copy-start | bytes 6148
  8.0 0.7 %copy-start.10 = (f32[1,4,6]{2,1,0:T(4,128)S(1)}, f32[1,4,6]{2,1,0:T(4,128)}, u32[]{:S(2)}) copy-start(f32[1,4,6]{2,1,0:T(4,128)} %param.27) | copy-start | bytes 292
